TPU v7x, 32 devices: a whole 2x2x4 slice. The times are simulated.
32 devices in a mesh: runs: 2 (over y), seg: 4 (over z), blk: 4 (over x, core).
Axes of the slice: x: 2, y: 2, z: 4, core: 2. Of those that a mesh axis runs over, the one named last changes fastest.
Arguments:
- bond_tensor: bfloat16 [8, 64, 64, 512], P(('runs', 'seg'), 'blk'), parts along dimension 0, may hold values from -36 to 36
- left_env: bfloat16 [8, 64, 64, 640], P(('runs', 'seg'), 'blk'), parts along dimension 0, may hold values from -0.75 to 0.75
- right_env: bfloat16 [8, 64, 64, 640], P(('runs', 'seg'), 'blk'), parts along dimension 0, may hold values from -0.25 to 0.25
- kept_dims: int32 [8, 2, 64], P(('runs', 'seg'), None, 'blk'), parts along dimension 0, may hold values from 16 to 64
- sector_links: int32 [8, 64, 10], P(('runs', 'seg'), 'blk'), parts along dimension 0, may hold values from -1 to 1
- mpo_pair: bfloat16 [80, 80], replicated, may hold values from -0.625 to 0.625
Outputs:
- handed_env: bfloat16 [8, 64, 64, 640], P(('runs', 'seg'), 'blk'), parts along dimension 0
There are 2 independent parts, one for each index of `runs`. A program takes and returns all parts, laid end to end along the dimension named above; an argument that names none is the same for every part. Nothing has to cross between parts.
All inputs are finite; a program needn't handle non-finite values.
Results may differ from a plain program's by a relative error of at most 0.0067.
Values may be sent and summed in bfloat16 or wider, within the bound.
A program may use at most 192 MiB of HBM per device.

v0:
```python
import math

import jax
import jax.numpy as jnp
from jax import lax
from jax.sharding import PartitionSpec as P

BS = 64
P_SIZE = 8
W = 10


relax_step = 0.5
epsilon = 1e-06


def padded_2(block, sides, width):
    for axis, dim in sides:
        count = lax.axis_size(axis)
        forward = [(i, i + 1) for i in range(count - 1)]
        backward = [(target, source) for source, target in forward]
        low = lax.ppermute(
            lax.slice_in_dim(block, block.shape[dim] - width, None, axis=dim), axis, forward
        )
        high = lax.ppermute(lax.slice_in_dim(block, 0, width, axis=dim), axis, backward)
        block = jnp.concatenate([low, block, high], axis=dim)
    return block


def from_behind(value, axis, by):
    devices = lax.axis_size(axis)
    return lax.ppermute(value, axis, [(i, (i + by) % devices) for i in range(devices)])


def lift_state(left_block, current, links):
    sect_dev = current.shape[0]
    padded = padded_2(current, (("blk", 0),), 1)
    source_idx = jnp.arange(sect_dev, dtype=jnp.int32)[:, None] + 1 + links
    picked = padded[source_idx]
    stacked = left_block.reshape(sect_dev, BS, W, BS)
    lifted = jnp.einsum("jawc,jwcn->jwan", stacked, picked, preferred_element_type=jnp.float32)
    return lifted.astype(jnp.bfloat16)


def solve_local(left_block, right_block, tensor_block, kept_block, links, mpo_pair):
    sect_dev = tensor_block.shape[0]
    total_count = sect_dev * lax.axis_size("blk") * BS * P_SIZE * BS
    positions = jnp.arange(BS, dtype=jnp.int32)[None, :]
    row_keep = (positions < kept_block[0][:, None]).astype(jnp.float32)
    col_keep = (positions < kept_block[1][:, None]).astype(jnp.float32)
    keep_mask = row_keep[:, :, None, None] * col_keep[:, None, None, :]
    current = (tensor_block.reshape(sect_dev, BS, P_SIZE, BS) * keep_mask).astype(jnp.bfloat16)
    current = current.reshape(sect_dev, BS, P_SIZE * BS)
    operator = mpo_pair.reshape(W, P_SIZE, W, P_SIZE)
    lifted = lift_state(left_block, current, links)
    channel_mix = jnp.einsum(
        "jwapb,wpvr->jarvb",
        lifted.reshape(sect_dev, W, BS, P_SIZE, BS),
        operator,
        preferred_element_type=jnp.float32,
    ).astype(jnp.bfloat16)
    channel_mix = channel_mix.reshape(sect_dev, BS, P_SIZE, W * BS)
    applied = jnp.einsum(
        "jarx,jcx->jarc", channel_mix, right_block, preferred_element_type=jnp.float32
    )
    applied = (applied * keep_mask).reshape(sect_dev, BS, P_SIZE * BS)
    trial_state = current.astype(jnp.float32) - relax_step * applied
    total = lax.psum(jnp.sum(trial_state * trial_state), "blk")
    current = (trial_state / jnp.sqrt(total / total_count + epsilon)).astype(jnp.bfloat16)
    closing = lift_state(left_block, current, links)
    handed = jnp.einsum(
        "japb,jwapc->jbwc",
        current.reshape(sect_dev, BS, P_SIZE, BS),
        closing.reshape(sect_dev, W, BS, P_SIZE, BS),
        preferred_element_type=jnp.float32,
    )
    handed = handed / math.sqrt(BS * P_SIZE)
    return handed.reshape(sect_dev, BS, W * BS).astype(jnp.bfloat16)


def shards(bond_tensor, left_env, right_env, kept_dims, sector_links, mpo_pair):
    right_block = from_behind(right_env, "seg", -1)
    handed = solve_local(
        left_env[0], right_block[0], bond_tensor[0], kept_dims[0], sector_links[0], mpo_pair
    )[None]
    result = from_behind(handed, "seg", 1)
    return result


def solution(mesh):
    return jax.shard_map(
        shards,
        mesh=mesh,
        in_specs=(
            P(("runs", "seg"), "blk", None, None),
            P(("runs", "seg"), "blk", None, None),
            P(("runs", "seg"), "blk", None, None),
            P(("runs", "seg"), None, "blk"),
            P(("runs", "seg"), "blk", None),
            P(),
        ),
        out_specs=P(("runs", "seg"), "blk", None, None),
        check_vma=False,
    )
```

profile of v0, /device:TPU:0, one launch (start us, length us, event | category | flops | bytes accessed | tf_op | source)
XLA Modules:
  0.0 276.4 jit_solution(13960001112776169989)
XLA Ops:
  0.0 0.8 slice_bitcast_fusion.1
  0.8 4.0 %reshape.144 = f32[16,64,8,64]{3,2,1,0:T(8,128)} reshape(bf16[1,16,64,512]{3,2,1,0:T(8,128)(2,1)} %param.6) | data formatting | bytes 3145728 | tf_op jit(solution)/shard_map/convert_element_type | solution.py:52
  4.8 0.1 fusion.11
  4.8 0.2 broadcast_multiply_fusion
  5.0 3.1 %fusion.5 = bf16[16,64,8,64]{3,1,2,0:T(8,128)(2,1)S(1)} fusion(f32[16,64,8,64]{3,2,1,0:T(8,128)} %reshape.144, f32[16,64,64]{2,1,0:T(8,128)S(1)} %broadcast_multiply_fusion), kind=kLoop, calls=%fused_computation.12 | loop fusion | flops 1048576 | bytes 3407872 | tf_op jit(solution)/shard_map/convert_element_type | solution.py:52
  8.1 0.0 copy-start.1
  8.2 1.3 copy-done.1
  9.5 0.1 copy.38
  9.6 0.1 slice.29
  9.8 2.4 collective-permute-start
  12.1 0.1 copy.40
  12.2 0.1 slice.31
  12.4 1.3 collective-permute-start.1
  13.7 4.5 %collective-permute-start.2 = (bf16[1,16,64,640]{3,2,1,0:T(8,128)(2,1)}, bf16[1,16,64,640]{3,2,1,0:T(8,128)(2,1)}, u32[]{:S(2)}, u32[]{:S(2)}) collective-permute-start(bf16[1,16,64,640]{3,2,1,0:T(8,128)(2,1)} %param.8), channel_id=1, source_target_pairs={{0,12},{4,0},{8,4},{12,8},{1,13},{5,1},{9,5},{13,9},{2,14},{6,2},{... | collective-permute-start | bytes 3932168 | tf_op jit(solution)/shard_map/ppermute | solution.py:32
  18.2 2.3 mul.57.clone
  20.4 0.0 copy-start
  20.4 0.0 copy-start.4
  20.4 4.9 %mul.59 = f32[16,64,512]{2,1,0:T(8,128)} reshape(f32[16,64,8,64]{3,2,1,0:T(8,128)} %mul.57.clone) | data formatting | bytes 4194304 | tf_op jit(solution)/shard_map/mul | solution.py:52
  25.3 0.0 copy-done
  25.3 0.0 copy-start.3
  25.3 1.9 fusion.9
  27.3 0.0 copy-done.4
  27.3 0.1 copy.41
  27.4 0.1 reshape.148
  27.5 3.8 %copy.42 = bf16[1,16,64,640]{2,3,1,0:T(8,128)(2,1)} copy(bf16[1,16,64,640]{3,2,1,0:T(8,128)(2,1)} %param.7) | data formatting | bytes 2621440 | tf_op args[1]
  31.2 0.0 copy-done.3
  31.2 0.3 reshape.141
  31.5 0.6 copy.56
  32.1 0.0 collective-permute-done
  32.1 0.0 collective-permute-done.1
  32.1 0.2 pad_maximum_fusion
  32.3 7.5 %gather_fusion = bf16[160,64,512]{2,1,0:T(8,128)(2,1)} fusion(bf16[18,64,512]{2,1,0:T(8,128)(2,1)S(1)} %pad_maximum_fusion, s32[1024]{0:T(1024)S(1)} %pad_clamp_fusion), kind=kCustom, calls=%fused_computation | custom fusion | bytes 20972160 | tf_op jit(solution)/shard_map/gather | solution.py:39
  39.8 8.9 %convert_bitcast_fusion.1 = bf16[16,10,64,512]{3,2,1,0:T(8,128)(2,1)} fusion(bf16[16,10,64,512]{3,2,1,0:T(8,128)(2,1)} %bitcast.74, bf16[16,64,10,64]{1,3,2,0:T(8,128)(2,1)} %bitcast.75), kind=kOutput, calls=%fused_computation.8 | convolution fusion | flops 676331520 | bytes 22282240 | tf_op jit(solution)/shard_map/jawc,jwcn->jwan/dot_general | solution.py:41
  48.7 26.2 %reshape.140 = bf16[16,10,64,8,64]{4,3,2,1,0:T(8,128)(2,1)} reshape(bf16[16,10,64,512]{3,2,1,0:T(8,128)(2,1)} %convert_bitcast_fusion.1) | data formatting | bytes 20971520 | tf_op jit(solution)/shard_map/reshape | solution.py:58
  74.9 20.9 %fusion = bf16[16,64,8,10,64]{4,3,2,1,0:T(8,128)(2,1)} fusion(bf16[10,8,10,8,1,1]{2,1,0,3,5,4:T(8,128)(2,1)S(1)} %copy.56, bf16[16,10,64,8,64]{4,3,2,1,0:T(8,128)(2,1)} %reshape.140), kind=kOutput, calls=%fused_computation.3 | convolution fusion | flops 844103680 | bytes 20984320 | tf_op jit(solution)/shard_map/jwapb,wpvr->jarvb/dot_general | solution.py:56
  95.8 43.2 %copy.46 = bf16[16,64,8,10,64]{1,4,3,2,0:T(8,128)(2,1)} copy(bf16[16,64,8,10,64]{4,3,2,1,0:T(8,128)(2,1)} %fusion) | data formatting | bytes 20971520 | tf_op jit(solution)/shard_map/convert_element_type | solution.py:61
  139.0 0.0 collective-permute-done.2
  139.0 12.9 %multiply_reduce_fusion = (f32[]{:T(128)}, f32[16,64,8,64]{3,1,2,0:T(8,128)}) fusion(bf16[16,64,8,64]{3,1,2,0:T(8,128)(2,1)} %copy-done.1, f32[16,64,64]{2,1,0:T(8,128)S(1)} %broadcast_multiply_fusion, bf16[16,64,8,640]{1,3,2,0:T(8,128)(2,1)} %bitcast.77, bf16[1,16,64,640]{3,2,1,0:T(8,128)(2,1)} %collective-permute-done.2), kind=kOutput, calls=%fused_computation.14 | convolution fusion | flops 674234368 | bytes 15204356 | tf_op jit(solution)/shard_map/jarx,jcx->jarc/dot_general | solution.py:63
  151.9 7.4 %copy.48 = f32[16,64,8,64]{3,2,1,0:T(8,128)} copy(f32[16,64,8,64]{3,1,2,0:T(8,128)} %get-tuple-element.12) | data formatting | bytes 4194304 | tf_op jit(solution)/shard_map/mul | solution.py:67
  159.4 4.8 %mul.65 = f32[16,64,512]{2,1,0:T(8,128)} reshape(f32[16,64,8,64]{3,2,1,0:T(8,128)} %copy.48) | data formatting | bytes 4194304 | tf_op jit(solution)/shard_map/mul | solution.py:67
  164.1 8.3 %psum.7 = f32[]{:T(128)} all-reduce(f32[]{:T(128)} %get-tuple-element.11), channel_id=1, replica_groups=mesh['runs'=2,'seg'=4,'blk'=4] {'blk'}, use_global_device_ids=true, to_apply=%region_1.0 | all-reduce | flops 1 | bytes 8 | tf_op jit(solution)/shard_map/psum | solution.py:68
  173.2 2.0 divide_convert_fusion.1
  175.2 2.0 collective-permute-start.3
  177.2 1.3 collective-permute-start.4
  178.5 0.0 collective-permute-done.3
  178.5 3.3 %collective-permute-done.4 = bf16[1,64,512]{2,1,0:T(8,128)(2,1)S(1)} collective-permute-done((bf16[1,64,512]{2,1,0:T(8,128)(2,1)S(1)}, bf16[1,64,512]{2,1,0:T(8,128)(2,1)S(1)}, u32[]{:S(2)}, u32[]{:S(2)}) %collective-permute-start.4) | collective-permute-done | bytes 65568 | tf_op jit(solution)/shard_map/ppermute | solution.py:25
  181.8 0.2 pad_maximum_fusion.1
  182.0 7.6 %gather_fusion.1 = bf16[160,64,512]{2,1,0:T(8,128)(2,1)} fusion(bf16[18,64,512]{2,1,0:T(8,128)(2,1)S(1)} %pad_maximum_fusion.1, s32[1024]{0:T(1024)S(1)} %pad_clamp_fusion), kind=kCustom, calls=%fused_computation.1 | custom fusion | bytes 20972160 | tf_op jit(solution)/shard_map/gather | solution.py:39
  189.6 8.9 %convert_bitcast_fusion = bf16[16,10,64,512]{3,2,1,0:T(8,128)(2,1)} fusion(bf16[16,10,64,512]{3,2,1,0:T(8,128)(2,1)} %bitcast.73, bf16[16,64,10,64]{1,3,2,0:T(8,128)(2,1)} %bitcast.76), kind=kOutput, calls=%fused_computation.7 | convolution fusion | flops 676331520 | bytes 22282240 | tf_op jit(solution)/shard_map/jawc,jwcn->jwan/dot_general | solution.py:41
  198.5 0.0 copy-start.2
  198.5 26.3 %reshape.143 = bf16[16,10,64,8,64]{4,3,2,1,0:T(8,128)(2,1)} reshape(bf16[16,10,64,512]{3,2,1,0:T(8,128)(2,1)} %convert_bitcast_fusion) | data formatting | bytes 20971520 | tf_op jit(solution)/shard_map/reshape | solution.py:74
  224.9 0.0 copy-done.2
  224.9 12.8 %fusion.4 = bf16[16,64,10,64]{3,1,2,0:T(8,128)(2,1)} fusion(bf16[16,10,64,8,64]{4,3,2,1,0:T(8,128)(2,1)} %reshape.143, f32[16,64,8,64]{3,1,2,0:T(8,128)} %get-tuple-element.12, bf16[16,64,8,64]{3,1,2,0:T(8,128)(2,1)S(1)} %copy-done.2, f32[]{:T(128)S(6)} %sqrt.3), kind=kOutput, calls=%fused_computation.10 | convolution fusion | flops 674496512 | bytes 14942212 | tf_op jit(solution)/shard_map/japb,jwapc->jbwc/dot_general | solution.py:71
  237.6 3.2 %copy.52 = bf16[16,64,10,64]{1,3,2,0:T(8,128)(2,1)S(1)} copy(bf16[16,64,10,64]{3,1,2,0:T(8,128)(2,1)} %fusion.4) | data formatting | bytes 2621440 | tf_op jit(solution)/shard_map/convert_element_type | solution.py:78
  240.8 2.9 %copy.53 = bf16[1,16,64,640]{3,2,1,0:T(8,128)(2,1)} copy(bf16[1,16,64,640]{2,3,1,0:T(8,128)(2,1)S(1)} %bitcast.78) | data formatting | bytes 2621440 | tf_op jit(solution)/shard_map/convert_element_type | solution.py:78
  243.8 0.0 collective-permute-start.5
  243.8 31.6 %collective-permute-done.5 = bf16[1,16,64,640]{3,2,1,0:T(8,128)(2,1)S(1)} collective-permute-done((bf16[1,16,64,640]{3,2,1,0:T(8,128)(2,1)}, bf16[1,16,64,640]{3,2,1,0:T(8,128)(2,1)S(1)}, u32[]{:S(2)}, u32[]{:S(2)}) %collective-permute-start.5) | collective-permute-done | bytes 1310752 | tf_op jit(solution)/shard_map/ppermute | solution.py:32
  275.4 1.1 copy.80
  (5 shorter events, 0.0 us)
Async XLA Ops:
  8.1 1.4 copy-start.1
  9.8 22.3 %collective-permute-start = (bf16[1,64,512]{2,1,0:T(8,128)(2,1)S(1)}, bf16[1,64,512]{2,1,0:T(8,128)(2,1)S(1)}, u32[]{:S(2)}, u32[]{:S(2)}) collective-permute-start(bf16[1,64,512]{2,1,0:T(8,128)(2,1)S(1)} %slice.29), channel_id=1, source_target_pairs={{0,1},{1,2},{2,3},{4,5},{5,6},{6,7},{8,9},{9,10},{10,11},{12,13},{... | collective-permute-start | bytes 196616 | tf_op jit(solution)/shard_map/ppermute | solution.py:22
  12.4 19.7 %collective-permute-start.1 = (bf16[1,64,512]{2,1,0:T(8,128)(2,1)S(1)}, bf16[1,64,512]{2,1,0:T(8,128)(2,1)S(1)}, u32[]{:S(2)}, u32[]{:S(2)}) collective-permute-start(bf16[1,64,512]{2,1,0:T(8,128)(2,1)S(1)} %slice.31), channel_id=1, source_target_pairs={{1,0},{2,1},{3,2},{5,4},{6,5},{7,6},{9,8},{10,9},{11,10},{13,12},{... | collective-permute-start | bytes 196616 | tf_op jit(solution)/shard_map/ppermute | solution.py:25
  13.7 125.4 %collective-permute-start.2 = (bf16[1,16,64,640]{3,2,1,0:T(8,128)(2,1)}, bf16[1,16,64,640]{3,2,1,0:T(8,128)(2,1)}, u32[]{:S(2)}, u32[]{:S(2)}) collective-permute-start(bf16[1,16,64,640]{3,2,1,0:T(8,128)(2,1)} %param.8), channel_id=1, source_target_pairs={{0,12},{4,0},{8,4},{12,8},{1,13},{5,1},{9,5},{13,9},{2,14},{6,2},{... | collective-permute-start | bytes 3932168 | tf_op jit(solution)/shard_map/ppermute | solution.py:32
  20.4 4.9 %copy-start = (bf16[1,16,64,512]{3,2,1,0:T(8,128)(2,1)S(1)}, bf16[1,16,64,512]{3,2,1,0:T(8,128)(2,1)}, u32[]{:S(2)}) copy-start(bf16[1,16,64,512]{3,2,1,0:T(8,128)(2,1)} %param.6) | copy-start | bytes 3145732
  20.4 6.8 %copy-start.4 = (s32[1,16,10]{1,0,2:T(1,128)S(1)}, s32[1,16,10]{1,0,2:T(1,128)}, u32[]{:S(2)}) copy-start(s32[1,16,10]{1,0,2:T(1,128)} %param.10) | copy-start | bytes 1924
  25.3 5.9 %copy-start.3 = (bf16[80,80]{1,0:T(8,128)(2,1)S(1)}, bf16[80,80]{1,0:T(8,128)(2,1)}, u32[]{:S(2)}) copy-start(bf16[80,80]{1,0:T(8,128)(2,1)} %param.11) | copy-start | bytes 38404
  175.2 3.4 %collective-permute-start.3 = (bf16[1,64,512]{2,1,0:T(8,128)(2,1)S(1)}, bf16[1,64,512]{2,1,0:T(8,128)(2,1)S(1)}, u32[]{:S(2)}, u32[]{:S(2)}) collective-permute-start(bf16[1,64,512]{2,1,0:T(8,128)(2,1)S(1)} %get-tuple-element.7), channel_id=1, source_target_pairs={{0,1},{1,2},{2,3},{4,5},{5,6},{6,7},{8,9},{9,10},{10,11},{12,13},{... | collective-permute-start | bytes 196616 | tf_op jit(solution)/shard_map/ppermute | solution.py:22
  177.2 4.6 %collective-permute-start.4 = (bf16[1,64,512]{2,1,0:T(8,128)(2,1)S(1)}, bf16[1,64,512]{2,1,0:T(8,128)(2,1)S(1)}, u32[]{:S(2)}, u32[]{:S(2)}) collective-permute-start(bf16[1,64,512]{2,1,0:T(8,128)(2,1)S(1)} %get-tuple-element.8), channel_id=1, source_target_pairs={{1,0},{2,1},{3,2},{5,4},{6,5},{7,6},{9,8},{10,9},{11,10},{13,12},{... | collective-permute-start | bytes 196616 | tf_op jit(solution)/shard_map/ppermute | solution.py:25
  198.5 26.3 %copy-start.2 = (bf16[16,64,8,64]{3,1,2,0:T(8,128)(2,1)S(1)}, bf16[16,64,8,64]{3,1,2,0:T(8,128)(2,1)}, u32[]{:S(2)}) copy-start(bf16[16,64,8,64]{3,1,2,0:T(8,128)(2,1)} %copy-done.1) | copy-start | bytes 3145732
  243.8 31.6 %collective-permute-start.5 = (bf16[1,16,64,640]{3,2,1,0:T(8,128)(2,1)}, bf16[1,16,64,640]{3,2,1,0:T(8,128)(2,1)S(1)}, u32[]{:S(2)}, u32[]{:S(2)}) collective-permute-start(bf16[1,16,64,640]{3,2,1,0:T(8,128)(2,1)} %copy.53), channel_id=1, source_target_pairs={{0,4},{4,8},{8,12},{12,0},{1,5},{5,9},{9,13},{13,1},{2,6},{6,10},{... | collective-permute-start | bytes 3932168 | tf_op jit(solution)/shard_map/ppermute | solution.py:32
where the time goes:
time: 281 us; the launch traced here: 276 us
  local copies, waits for them, and re-layouts  149 us (53%)
  matrix products  64.4 us (23%)
  waiting for transfers between devices  35 us (12%)
  starting transfers between devices  11.5 us (4%)
  blocking collectives  8.34 us (3%)
  other arithmetic  7.6 us (3%)
    convert_element_type x1, local copies, waits for them, and re-layouts, solve_local(): channel_mix = jnp.einsum('jwapb,wpvr->jarvb', lifted.reshape(sect_dev, W,...  43.2 us
    ppermute x2, waiting for transfers between devices, from_behind(): lax.ppermute(value, axis, [(i, (i + by) % devices) for i in range(devices)])  31.6 us
    reshape x1, local copies, waits for them, and re-layouts, solve_local(): closing.reshape(sect_dev, W, BS, P_SIZE, BS)  26.3 us
    reshape x1, local copies, waits for them, and re-layouts, solve_local(): lifted.reshape(sect_dev, W, BS, P_SIZE, BS)  26.2 us
    dot_general x1, matrix products, solve_local(): jnp.einsum('jwapb,wpvr->jarvb', lifted.reshape(sect_dev, W, BS, P_SIZE, B...  20.9 us
    dot_general x2, matrix products, lift_state(): jnp.einsum('jawc,jwcn->jwan', stacked, picked, preferred_element_type=jnp...  17.8 us
    gather x2, local copies, waits for them, and re-layouts, lift_state(): picked = padded[source_idx]  15.1 us
    dot_general x1, matrix products, solve_local(): jnp.einsum('jarx,jcx->jarc', channel_mix, right_block, preferred_element_...  12.9 us
  transfers between devices with their start and end apart: 6, of which 2 were waited for; matrix products, arithmetic and copies ran while one was open for 44% of the time, Pallas kernels for 0%

commit v1 on v0

v1 whole, which is shorter than its diff:
```python
import math

import jax
import jax.numpy as jnp
from jax import lax
from jax.experimental import pallas as pl
from jax.experimental.pallas import tpu as pltpu
from jax.sharding import PartitionSpec as P

BS = 64
P_SIZE = 8
W = 10
LANES = P_SIZE * BS
WIDE = W * BS
MIX = W * 128

relax_step = 0.5
epsilon = 1e-06
lift_scale = 1024.0

f32 = jnp.float32
bf16 = jnp.bfloat16


def iota(shape, dim):
    return lax.broadcasted_iota(jnp.int32, shape, dim)


def dot(a, b, dims=((1,), (0,))):
    return lax.dot_general(a, b, (dims, ((), ())), preferred_element_type=f32)


def order_state(order_ref):
    row, lane = iota((LANES, LANES), 0), iota((LANES, LANES), 1)
    source = ((lane >> 4) & 7) * 64 + (lane >> 7) * 16 + (lane & 15)
    order_ref[...] = (row == source).astype(f32).astype(bf16)


def order_right(order_ref):
    row, lane = iota((WIDE, 128), 0), iota((WIDE, 128), 1)
    for b_hi in range(4):
        for v_hi in range(5):
            source = (v_hi * 2 + ((lane >> 4) & 1)) * 64 + b_hi * 16 + (lane & 15)
            at = (b_hi * 5 + v_hi) * 128
            order_ref[:, at : at + 128] = (row == source).astype(f32).astype(bf16)


def spread_operator(mpo_ref, mix_ref):
    size = W * P_SIZE
    rows = (iota((MIX, size), 1) == (iota((MIX, size), 0) >> 4)).astype(f32).astype(bf16)
    tall = dot(rows, mpo_ref[...]).astype(bf16)
    same = (iota((MIX, 128), 0) & 15) == (iota((MIX, 128), 1) & 15)
    row, lane = iota((size, 128), 0), iota((size, 128), 1)
    for r_hi in range(2):
        for v_hi in range(5):
            column = (v_hi * 2 + ((lane >> 4) & 1)) * 8 + r_hi * 4 + ((lane >> 5) & 3)
            pick = (row == column).astype(f32).astype(bf16)
            at = (r_hi * 5 + v_hi) * 128
            mix_ref[:, at : at + 128] = jnp.where(same, dot(tall, pick), 0.0).astype(bf16)


def keep_of(kept_ref, q, lanes):
    rows = iota((BS, lanes), 0) < kept_ref[0, q]
    columns = (iota((BS, lanes), 1) & 63) < kept_ref[1, q]
    return rows & columns


def lift_into(links_ref, q, left, state_ref, target_ref):
    for w in range(W):
        source = state_ref[q + 1 + links_ref[q, w]]
        out = dot(left[:, w * 64 : w * 64 + 64], source).astype(bf16)
        for k in range(4):
            target_ref[k * 64 : k * 64 + 64, w * 128 : w * 128 + 128] = out[:, k * 128 : k * 128 + 128]


def relax_sector(links_ref, kept_ref, q, left, right, bond, ordered_ref, order_ref, mix_ref, x_ref, rk_ref):
    lift_into(links_ref, q, left, ordered_ref, x_ref)
    mixed = dot(x_ref[...], mix_ref[...]).astype(bf16)
    spread = dot(right, order_ref[...]).astype(bf16)
    part = (iota((BS, 4 * WIDE), 1) >> 5) & 3
    for k in range(4):
        rk_ref[k * 64 : k * 64 + 64, :] = jnp.where(part == k, spread, jnp.zeros_like(spread))
    keep = keep_of(kept_ref, q, 256)
    halves = []
    for r_hi in range(2):
        rows = jnp.concatenate(
            [mixed[k * 64 : k * 64 + 64, r_hi * WIDE : r_hi * WIDE + WIDE] for k in range(4)], axis=1
        )
        applied = dot(rows, rk_ref[...], ((1,), (1,)))
        state = bond[:, r_hi * 256 : r_hi * 256 + 256].astype(f32)
        halves.append(jnp.where(keep, state - relax_step * applied, 0.0))
    return halves


def handed_sector(links_ref, q, left, state_ref, x_ref):
    lift_into(links_ref, q, left, state_ref, x_ref)
    own = state_ref[q + 1]
    stacked = jnp.concatenate([own[:, k * 128 : k * 128 + 128] for k in range(4)], axis=0)
    both = dot(stacked, x_ref[...], ((0,), (0,)))
    low = iota((BS, 128), 1) < 64
    out = []
    for w in range(0, W, 2):
        a0, b0 = both[:64, w * 128 : w * 128 + 128], both[64:, w * 128 : w * 128 + 128]
        a1, b1 = both[:64, w * 128 + 128 : w * 128 + 256], both[64:, w * 128 + 128 : w * 128 + 256]
        out.append(jnp.where(low, a0, b1) + pltpu.roll(jnp.where(low, a1, b0), 64, 1))
    return jnp.concatenate(out, axis=1)


def relax_kernel(links_ref, kept_ref, left_ref, right_ref, bond_ref, mpo_ref, state_ref, total_ref,
                 ordered_ref, lane_ref, order_ref, mix_ref, x_ref, rk_ref):
    step = pl.program_id(0)

    @pl.when(step == 0)
    def _():
        order_state(lane_ref)
        order_right(order_ref)
        spread_operator(mpo_ref, mix_ref)
        total_ref[...] = jnp.zeros_like(total_ref)

        def body(q, carry):
            keep = keep_of(kept_ref, q, LANES)
            held = jnp.where(keep, bond_ref[q].astype(f32), 0.0).astype(bf16)
            ordered_ref[q] = dot(held, lane_ref[...]).astype(bf16)
            return carry

        lax.fori_loop(0, bond_ref.shape[0], body, 0)

    halves = relax_sector(links_ref, ShiftedKept(kept_ref), step, left_ref[0], right_ref[0], bond_ref[step + 1],
                          ordered_ref, order_ref, mix_ref, x_ref, rk_ref)
    for r_hi, trial in enumerate(halves):
        total_ref[...] += trial * trial
        state_ref[0, :, r_hi * 256 : r_hi * 256 + 256] = (trial * lift_scale).astype(bf16)


class ShiftedKept:
    def __init__(self, ref):
        self.ref = ref

    def __getitem__(self, at):
        return self.ref[at[0], at[1] + 1]


def handed_kernel(links_ref, scale_ref, left_ref, state_ref, out_ref, x_ref):
    step = pl.program_id(0)
    value = handed_sector(links_ref, step, left_ref[0], state_ref, x_ref)
    out_ref[0] = (value * scale_ref[0, 0]).astype(bf16)


def padded(block, dim):
    count = lax.axis_size("blk")
    forward = [(i, i + 1) for i in range(count - 1)]
    backward = [(target, source) for source, target in forward]
    size = block.shape[dim]
    low = lax.ppermute(lax.slice_in_dim(block, size - 1, None, axis=dim), "blk", forward)
    high = lax.ppermute(lax.slice_in_dim(block, 0, 1, axis=dim), "blk", backward)
    return jnp.concatenate([low, block, high], axis=dim)


def shards(bond_tensor, left_env, right_env, kept_dims, sector_links, mpo_pair):
    count = lax.axis_size("seg")
    ring = [(i, (i + 1) % count) for i in range(count)]
    bond = padded(lax.ppermute(bond_tensor[0], "seg", ring), 0)
    left = lax.ppermute(left_env[0], "seg", ring)
    kept = padded(lax.ppermute(kept_dims[0], "seg", ring), 1)
    links = lax.ppermute(sector_links[0], "seg", ring)
    right = right_env[0]
    sectors = left.shape[0]
    smem = pl.BlockSpec(memory_space=pltpu.SMEM)
    per_sector = pl.BlockSpec((1, BS, WIDE), lambda q: (q, 0, 0))
    whole = pl.BlockSpec((sectors + 2, BS, LANES), lambda q: (0, 0, 0))
    params = pltpu.CompilerParams(vmem_limit_bytes=40 * 2**20)
    state, total = pl.pallas_call(
        relax_kernel,
        grid=(sectors,),
        out_shape=(jax.ShapeDtypeStruct((sectors, BS, LANES), bf16), jax.ShapeDtypeStruct((BS, 256), f32)),
        in_specs=[smem, smem, per_sector, per_sector, whole, pl.BlockSpec((80, 80), lambda q: (0, 0))],
        out_specs=(pl.BlockSpec((1, BS, LANES), lambda q: (q, 0, 0)), pl.BlockSpec((BS, 256), lambda q: (0, 0))),
        scratch_shapes=[
            pltpu.VMEM((sectors + 2, BS, LANES), bf16),
            pltpu.VMEM((LANES, LANES), bf16),
            pltpu.VMEM((WIDE, 4 * WIDE), bf16),
            pltpu.VMEM((MIX, MIX), bf16),
            pltpu.VMEM((256, MIX), bf16),
            pltpu.VMEM((256, 4 * WIDE), bf16),
        ],
        compiler_params=params,
    )(links, kept, left, right, bond, mpo_pair)
    total_count = sectors * lax.axis_size("blk") * BS * P_SIZE * BS
    mean_square = lax.psum(jnp.sum(total), "blk") / total_count
    scale = 1.0 / ((mean_square + epsilon) * (lift_scale * lift_scale * math.sqrt(BS * P_SIZE)))
    out = pl.pallas_call(
        handed_kernel,
        grid=(sectors,),
        out_shape=jax.ShapeDtypeStruct((sectors, BS, WIDE), bf16),
        in_specs=[smem, smem, per_sector, whole],
        out_specs=per_sector,
        scratch_shapes=[pltpu.VMEM((256, MIX), bf16)],
        compiler_params=params,
    )(links, scale.reshape(1, 1), left, padded(state, 0))
    return out[None]


def solution(mesh):
    return jax.shard_map(
        shards,
        mesh=mesh,
        in_specs=(
            P(("runs", "seg"), "blk", None, None),
            P(("runs", "seg"), "blk", None, None),
            P(("runs", "seg"), "blk", None, None),
            P(("runs", "seg"), None, "blk"),
            P(("runs", "seg"), "blk", None),
            P(),
        ),
        out_specs=P(("runs", "seg"), "blk", None, None),
        check_vma=False,
    )
```

time: 281 us -> 145 us (0.52); the launches traced: 276 us -> 145 us
  local copies, waits for them, and re-layouts: 149 us -> 0.86 us
  matrix products: 64.4 us -> 0 us
  Pallas kernels: 0 us -> 60.8 us
  waiting for transfers between devices: 35 us -> 52.7 us
  starting transfers between devices: 11.5 us -> 21 us
  other arithmetic: 7.6 us -> 0.99 us
    dot_general x5 -> x0, matrix products: 64.4 us -> none  [the longest x1 20.9 us: solve_local(): jnp.einsum('jwapb,wpvr->jarvb', lifted.reshape(sect_dev, W, BS, P_SIZE, B...]
    pallas_call x0 -> x2, Pallas kernels: none -> 60.8 us  [the longest x1 48.9 us: shards(): pl.pallas_call(relax_kernel, grid=(sectors,), out_shape=(jax.ShapeDtypeSt...]
    reshape x4 -> x0, local copies, waits for them, and re-layouts: 53.4 us -> none  [the longest x1 26.3 us: solve_local(): closing.reshape(sect_dev, W, BS, P_SIZE, BS)]
    convert_element_type x4 -> x0, local copies, waits for them, and re-layouts: 53.3 us -> none  [the longest x1 43.2 us: solve_local(): channel_mix = jnp.einsum('jwapb,wpvr->jarvb', lifted.reshape(sect_dev, W,...]
    mul x4 -> x0, local copies, waits for them, and re-layouts: 19.3 us -> none  [the longest x2 12.2 us: solve_local(): trial_state = current.astype(jnp.float32) - relax_step * applied]
    ppermute x6 -> x10, waiting for transfers between devices: 35 us -> 52.7 us  [the longest x1 49.7 us: shards(): kept = padded(lax.ppermute(kept_dims[0], 'seg', ring), 1)]
    gather x2 -> x0, local copies, waits for them, and re-layouts: 15.1 us -> none  [lift_state(): picked = padded[source_idx]]
    ppermute x6 -> x10, starting transfers between devices: 11.5 us -> 21 us  [the longest x3 10.9 us: padded(): lax.ppermute(lax.slice_in_dim(block, size - 1, None, axis=dim), 'blk', fo...]
  transfers between devices with their start and end apart: 6 -> 10, of which waited for: 2 -> 2; matrix products, arithmetic and copies ran while one was open for 44% -> 1% of each run, Pallas kernels for 0% -> 0%
where the time goes in v1:
time: 145 us
  Pallas kernels  60.8 us (42%)
  waiting for transfers between devices  52.7 us (36%)
  starting transfers between devices  21 us (14%)
  blocking collectives  7.38 us (5%)
    ppermute x1, waiting for transfers between devices, shards(): kept = padded(lax.ppermute(kept_dims[0], 'seg', ring), 1)  49.7 us
    pallas_call x1, Pallas kernels, shards(): pl.pallas_call(relax_kernel, grid=(sectors,), out_shape=(jax.ShapeDtypeSt...  48.9 us
    pallas_call x1, Pallas kernels, shards(): pl.pallas_call(handed_kernel, grid=(sectors,), out_shape=jax.ShapeDtypeSt...  11.9 us
    ppermute x3, starting transfers between devices, padded(): lax.ppermute(lax.slice_in_dim(block, size - 1, None, axis=dim), 'blk', fo...  10.9 us
    psum x1, blocking collectives, shards(): mean_square = lax.psum(jnp.sum(total), 'blk') / total_count  7.38 us
    ppermute x3, starting transfers between devices, padded(): lax.ppermute(lax.slice_in_dim(block, 0, 1, axis=dim), 'blk', backward)  3.88 us
    ppermute x1, starting transfers between devices, shards(): bond = padded(lax.ppermute(bond_tensor[0], 'seg', ring), 0)  3.02 us
    ppermute x3, waiting for transfers between devices, padded(): lax.ppermute(lax.slice_in_dim(block, 0, 1, axis=dim), 'blk', backward)  2.99 us
  transfers between devices with their start and end apart: 10, of which 2 were waited for; matrix products, arithmetic and copies ran while one was open for 1% of the time, Pallas kernels for 0%

profile of v1, /device:TPU:0, one launch (start us, length us, event | category | flops | bytes accessed | tf_op | source)
XLA Modules:
  0.0 144.6 jit_solution(11420187912709411422)
XLA Ops:
  0.0 3.0 %collective-permute-start.5 = (bf16[16,64,512]{2,1,0:T(8,128)(2,1)}, bf16[16,64,512]{2,1,0:T(8,128)(2,1)S(1)}, u32[]{:S(2)}, u32[]{:S(2)}) collective-permute-start(bf16[16,64,512]{2,1,0:T(8,128)(2,1)} %bitcast.10), channel_id=1, source_target_pairs={{0,4},{4,8},{8,12},{12,0},{1,5},{5,9},{9,13},{13,1},{2,6},{6,10},{... | collective-permute-start | bytes 3145736 | tf_op jit(solution)/shard_map/ppermute | solution.py:162
  3.0 1.6 %collective-permute-start.4 = (bf16[16,64,640]{2,1,0:T(8,128)(2,1)}, bf16[16,64,640]{2,1,0:T(8,128)(2,1)S(1)}, u32[]{:S(2)}, u32[]{:S(2)}) collective-permute-start(bf16[16,64,640]{2,1,0:T(8,128)(2,1)} %bitcast.9), channel_id=1, source_target_pairs={{0,4},{4,8},{8,12},{12,0},{1,5},{5,9},{9,13},{13,1},{2,6},{6,10},{... | collective-permute-start | bytes 3932168 | tf_op jit(solution)/shard_map/ppermute | solution.py:163
  4.6 1.6 %collective-permute-start.1 = (s32[2,16]{1,0:T(2,128)}, s32[2,16]{1,0:T(2,128)S(1)}, u32[]{:S(2)}, u32[]{:S(2)}) collective-permute-start(s32[2,16]{1,0:T(2,128)} %bitcast.11), channel_id=1, source_target_pairs={{0,4},{4,8},{8,12},{12,0},{1,5},{5,9},{9,13},{13,1},{2,6},{6,10},{... | collective-permute-start | bytes 392 | tf_op jit(solution)/shard_map/ppermute | solution.py:164
  6.2 0.8 copy.7
  6.9 0.0 collective-permute-start
  7.0 49.7 %collective-permute-done.1 = s32[2,16]{1,0:T(2,128)S(1)} collective-permute-done((s32[2,16]{1,0:T(2,128)}, s32[2,16]{1,0:T(2,128)S(1)}, u32[]{:S(2)}, u32[]{:S(2)}) %collective-permute-start.1) | collective-permute-done | bytes 160 | tf_op jit(solution)/shard_map/ppermute | solution.py:164
  56.7 0.1 fusion.2
  56.7 1.3 collective-permute-start.2
  58.0 1.3 collective-permute-start.3
  59.3 0.0 collective-permute-done.5
  59.3 4.8 %collective-permute-start.6 = (bf16[1,64,512]{2,1,0:T(8,128)(2,1)S(1)}, bf16[1,64,512]{2,1,0:T(8,128)(2,1)S(1)}, u32[]{:S(2)}, u32[]{:S(2)}) collective-permute-start(bf16[1,64,512]{2,1,0:T(8,128)(2,1)S(1)} %get-tuple-element.11), channel_id=1, source_target_pairs={{0,1},{1,2},{2,3},{4,5},{5,6},{6,7},{8,9},{9,10},{10,11},{12,13},{... | collective-permute-start | bytes 196616 | tf_op jit(solution)/shard_map/ppermute | solution.py:154
  64.1 0.0 collective-permute-done.2
  64.1 1.3 collective-permute-start.7
  65.4 0.0 collective-permute-done.3
  65.4 0.1 pad_add_fusion.kept_ref
  65.5 0.0 copy-start
  65.5 0.0 copy-start.1
  65.5 0.0 collective-permute-done.6
  65.5 3.0 %collective-permute-done.7 = bf16[1,64,512]{2,1,0:T(8,128)(2,1)S(1)} collective-permute-done((bf16[1,64,512]{2,1,0:T(8,128)(2,1)S(1)}, bf16[1,64,512]{2,1,0:T(8,128)(2,1)S(1)}, u32[]{:S(2)}, u32[]{:S(2)}) %collective-permute-start.7) | collective-permute-done | bytes 65568 | tf_op jit(solution)/shard_map/ppermute | solution.py:155
  68.5 0.2 pad_maximum_fusion.bond_ref
  68.7 0.0 collective-permute-done.links_ref
  68.7 0.0 collective-permute-done.4.left_ref
  68.7 0.0 copy-done
  68.7 0.0 copy-done.1
  68.7 48.9 %shard_map.64 = (bf16[16,64,512]{2,1,0:T(8,128)(2,1)S(1)}, f32[64,256]{1,0:T(8,128)S(1)}) custom-call(s32[16,10]{1,0:T(8,128)S(1)} %collective-permute-done.links_ref, s32[2,18]{1,0:T(2,128)S(1)} %pad_add_fusion.kept_ref, bf16[16,64,640]{2,1,0:T(8,128)(2,1)S(1)} %collective-permute-done.4.left_ref, bf16[16,64,640]{2,1,0:T(8,128)(2,1)S(1)} %bitcast.7, ...), custom_call_target="tpu_custom_call" | custom-call | tf_op jit(solution)/shard_map/pallas_call | solution.py:172
  117.7 4.8 %collective-permute-start.8 = (bf16[1,64,512]{2,1,0:T(8,128)(2,1)S(1)}, bf16[1,64,512]{2,1,0:T(8,128)(2,1)S(1)}, u32[]{:S(2)}, u32[]{:S(2)}) collective-permute-start(bf16[1,64,512]{2,1,0:T(8,128)(2,1)S(1)} %get-tuple-element.9), channel_id=1, source_target_pairs={{0,1},{1,2},{2,3},{4,5},{5,6},{6,7},{8,9},{9,10},{10,11},{12,13},{... | collective-permute-start | bytes 196616 | tf_op jit(solution)/shard_map/ppermute | solution.py:154
  122.5 1.3 collective-permute-start.9
  123.8 0.6 reduce_sum.9
  124.4 7.4 %psum.7 = f32[]{:T(128)} all-reduce(f32[]{:T(128)} %reduce_sum.9), channel_id=1, replica_groups=mesh['runs'=2,'seg'=4,'blk'=4] {'blk'}, use_global_device_ids=true, to_apply=%region_1.0 | all-reduce | flops 1 | bytes 8 | tf_op jit(solution)/shard_map/psum | solution.py:189
  132.5 0.0 collective-permute-done.8
  132.5 0.0 collective-permute-done.9
  132.5 0.2 pad_maximum_fusion.1.state_ref
  132.7 11.9 %shard_map.65 = bf16[16,64,640]{2,1,0:T(8,128)(2,1)} custom-call(s32[16,10]{1,0:T(8,128)S(1)} %collective-permute-done.links_ref, f32[1,1]{1,0:T(1,128)} %bitcast.5.scale_ref, bf16[16,64,640]{2,1,0:T(8,128)(2,1)S(1)} %collective-permute-done.4.left_ref, bf16[18,64,512]{2,1,0:T(8,128)(2,1)S(1)} %pad_maximum_fusion.1.state_ref), custom_call_target="tpu_custom_call" | custom-call | tf_op jit(solution)/shard_map/pallas_call | solution.py:191
  (2 shorter events, 0.0 us)
Async XLA Ops:
  0.0 59.3 %collective-permute-start.5 = (bf16[16,64,512]{2,1,0:T(8,128)(2,1)}, bf16[16,64,512]{2,1,0:T(8,128)(2,1)S(1)}, u32[]{:S(2)}, u32[]{:S(2)}) collective-permute-start(bf16[16,64,512]{2,1,0:T(8,128)(2,1)} %bitcast.10), channel_id=1, source_target_pairs={{0,4},{4,8},{8,12},{12,0},{1,5},{5,9},{9,13},{13,1},{2,6},{6,10},{... | collective-permute-start | bytes 3145736 | tf_op jit(solution)/shard_map/ppermute | solution.py:162
  3.0 65.6 %collective-permute-start.4 = (bf16[16,64,640]{2,1,0:T(8,128)(2,1)}, bf16[16,64,640]{2,1,0:T(8,128)(2,1)S(1)}, u32[]{:S(2)}, u32[]{:S(2)}) collective-permute-start(bf16[16,64,640]{2,1,0:T(8,128)(2,1)} %bitcast.9), channel_id=1, source_target_pairs={{0,4},{4,8},{8,12},{12,0},{1,5},{5,9},{9,13},{13,1},{2,6},{6,10},{... | collective-permute-start | bytes 3932168 | tf_op jit(solution)/shard_map/ppermute | solution.py:163
  4.6 52.0 %collective-permute-start.1 = (s32[2,16]{1,0:T(2,128)}, s32[2,16]{1,0:T(2,128)S(1)}, u32[]{:S(2)}, u32[]{:S(2)}) collective-permute-start(s32[2,16]{1,0:T(2,128)} %bitcast.11), channel_id=1, source_target_pairs={{0,4},{4,8},{8,12},{12,0},{1,5},{5,9},{9,13},{13,1},{2,6},{6,10},{... | collective-permute-start | bytes 392 | tf_op jit(solution)/shard_map/ppermute | solution.py:164
  6.9 61.7 %collective-permute-start = (s32[16,10]{1,0:T(8,128)S(1)}, s32[16,10]{1,0:T(8,128)S(1)}, u32[]{:S(2)}, u32[]{:S(2)}) collective-permute-start(s32[16,10]{1,0:T(8,128)S(1)} %bitcast.8), channel_id=1, source_target_pairs={{0,4},{4,8},{8,12},{12,0},{1,5},{5,9},{9,13},{13,1},{2,6},{6,10},{... | collective-permute-start | bytes 1928 | tf_op jit(solution)/shard_map/ppermute | solution.py:165
  56.7 7.4 %collective-permute-start.2 = (s32[2,1]{1,0:T(2,128)S(1)}, s32[2,1]{1,0:T(2,128)S(1)}, u32[]{:S(2)}, u32[]{:S(2)}) collective-permute-start(s32[2,1]{1,0:T(2,128)S(1)} %get-tuple-element.13), channel_id=1, source_target_pairs={{0,1},{1,2},{2,3},{4,5},{5,6},{6,7},{8,9},{9,10},{10,11},{12,13},{... | collective-permute-start | bytes 32 | tf_op jit(solution)/shard_map/ppermute | solution.py:154
  58.0 7.4 %collective-permute-start.3 = (s32[2,1]{1,0:T(2,128)S(1)}, s32[2,1]{1,0:T(2,128)S(1)}, u32[]{:S(2)}, u32[]{:S(2)}) collective-permute-start(s32[2,1]{1,0:T(2,128)S(1)} %get-tuple-element.14), channel_id=1, source_target_pairs={{1,0},{2,1},{3,2},{5,4},{6,5},{7,6},{9,8},{10,9},{11,10},{13,12},{... | collective-permute-start | bytes 32 | tf_op jit(solution)/shard_map/ppermute | solution.py:155
  59.3 6.2 %collective-permute-start.6 = (bf16[1,64,512]{2,1,0:T(8,128)(2,1)S(1)}, bf16[1,64,512]{2,1,0:T(8,128)(2,1)S(1)}, u32[]{:S(2)}, u32[]{:S(2)}) collective-permute-start(bf16[1,64,512]{2,1,0:T(8,128)(2,1)S(1)} %get-tuple-element.11), channel_id=1, source_target_pairs={{0,1},{1,2},{2,3},{4,5},{5,6},{6,7},{8,9},{9,10},{10,11},{12,13},{... | collective-permute-start | bytes 196616 | tf_op jit(solution)/shard_map/ppermute | solution.py:154
  64.1 4.4 %collective-permute-start.7 = (bf16[1,64,512]{2,1,0:T(8,128)(2,1)S(1)}, bf16[1,64,512]{2,1,0:T(8,128)(2,1)S(1)}, u32[]{:S(2)}, u32[]{:S(2)}) collective-permute-start(bf16[1,64,512]{2,1,0:T(8,128)(2,1)S(1)} %get-tuple-element.12), channel_id=1, source_target_pairs={{1,0},{2,1},{3,2},{5,4},{6,5},{7,6},{9,8},{10,9},{11,10},{13,12},{... | collective-permute-start | bytes 196616 | tf_op jit(solution)/shard_map/ppermute | solution.py:155
  65.5 3.2 %copy-start = (bf16[1,16,64,640]{3,2,1,0:T(8,128)(2,1)S(1)}, bf16[1,16,64,640]{3,2,1,0:T(8,128)(2,1)}, u32[]{:S(2)}) copy-start(bf16[1,16,64,640]{3,2,1,0:T(8,128)(2,1)} %param.8) | copy-start | bytes 3932164
  65.5 3.2 %copy-start.1 = (bf16[80,80]{1,0:T(8,128)(2,1)S(1)}, bf16[80,80]{1,0:T(8,128)(2,1)}, u32[]{:S(2)}) copy-start(bf16[80,80]{1,0:T(8,128)(2,1)} %mpo_ref.1) | copy-start | bytes 38404
  117.7 14.8 %collective-permute-start.8 = (bf16[1,64,512]{2,1,0:T(8,128)(2,1)S(1)}, bf16[1,64,512]{2,1,0:T(8,128)(2,1)S(1)}, u32[]{:S(2)}, u32[]{:S(2)}) collective-permute-start(bf16[1,64,512]{2,1,0:T(8,128)(2,1)S(1)} %get-tuple-element.9), channel_id=1, source_target_pairs={{0,1},{1,2},{2,3},{4,5},{5,6},{6,7},{8,9},{9,10},{10,11},{12,13},{... | collective-permute-start | bytes 196616 | tf_op jit(solution)/shard_map/ppermute | solution.py:154
  122.5 10.0 %collective-permute-start.9 = (bf16[1,64,512]{2,1,0:T(8,128)(2,1)S(1)}, bf16[1,64,512]{2,1,0:T(8,128)(2,1)S(1)}, u32[]{:S(2)}, u32[]{:S(2)}) collective-permute-start(bf16[1,64,512]{2,1,0:T(8,128)(2,1)S(1)} %get-tuple-element.10), channel_id=1, source_target_pairs={{1,0},{2,1},{3,2},{5,4},{6,5},{7,6},{9,8},{10,9},{11,10},{13,12},{... | collective-permute-start | bytes 196616 | tf_op jit(solution)/shard_map/ppermute | solution.py:155

commit v2 on v1

v2 whole, which is shorter than its diff:
```python
import functools
import math

import jax
import jax.numpy as jnp
from jax import lax
from jax.experimental import pallas as pl
from jax.experimental.pallas import tpu as pltpu
from jax.sharding import PartitionSpec as P

BS = 64
P_SIZE = 8
W = 10
LANES = P_SIZE * BS
WIDE = W * BS
MIX = W * 128

relax_step = 0.5
epsilon = 1e-06
lift_scale = 1024.0

f32 = jnp.float32
bf16 = jnp.bfloat16


def iota(shape, dim):
    return lax.broadcasted_iota(jnp.int32, shape, dim)


def dot(a, b, dims=((1,), (0,))):
    return lax.dot_general(a, b, (dims, ((), ())), preferred_element_type=f32)


def order_state(order_ref):
    row, lane = iota((LANES, LANES), 0), iota((LANES, LANES), 1)
    source = ((lane >> 4) & 7) * 64 + (lane >> 7) * 16 + (lane & 15)
    order_ref[...] = (row == source).astype(f32).astype(bf16)


def order_right(order_ref):
    row, lane = iota((WIDE, 128), 0), iota((WIDE, 128), 1)
    for b_hi in range(4):
        for v_hi in range(5):
            source = (v_hi * 2 + ((lane >> 4) & 1)) * 64 + b_hi * 16 + (lane & 15)
            at = (b_hi * 5 + v_hi) * 128
            order_ref[:, at : at + 128] = (row == source).astype(f32).astype(bf16)


def spread_operator(mpo_ref, mix_ref):
    size = W * P_SIZE
    rows = (iota((MIX, size), 1) == (iota((MIX, size), 0) >> 4)).astype(f32).astype(bf16)
    tall = dot(rows, mpo_ref[...]).astype(bf16)
    same = (iota((MIX, 128), 0) & 15) == (iota((MIX, 128), 1) & 15)
    row, lane = iota((size, 128), 0), iota((size, 128), 1)
    for r_hi in range(2):
        for v_hi in range(5):
            column = (v_hi * 2 + ((lane >> 4) & 1)) * 8 + r_hi * 4 + ((lane >> 5) & 3)
            pick = (row == column).astype(f32).astype(bf16)
            at = (r_hi * 5 + v_hi) * 128
            mix_ref[:, at : at + 128] = jnp.where(same, dot(tall, pick), 0.0).astype(bf16)


def keep_of(meta_ref, q, lanes):
    rows = iota((BS, lanes), 0) < meta_ref[q, W]
    columns = (iota((BS, lanes), 1) & 63) < meta_ref[q, W + 1]
    return rows & columns


def lift_into(meta_ref, q, left, state_ref, target_ref, base=0):
    for w in range(W):
        source = state_ref[q + 1 + meta_ref[q, w]]
        out = dot(left[:, w * 64 : w * 64 + 64], source).astype(bf16)
        for k in range(4):
            target_ref[base + k * 64 : base + k * 64 + 64, w * 128 : w * 128 + 128] = out[:, k * 128 : k * 128 + 128]


def relax_pair(meta_ref, g, left_ref, spread_ref, bond_ref, ordered_ref, mix_ref, x_ref, y_ref, rk_ref, state_ref, total_ref):
    for i in range(2):
        q = g * 2 + i
        lift_into(meta_ref, q, left_ref[q], ordered_ref, x_ref, i * 256)
    y_ref[...] = dot(x_ref[...], mix_ref[...]).astype(bf16)
    for i in range(2):
        q = g * 2 + i
        spread = spread_ref[q]
        part = (iota((BS, 4 * WIDE), 1) >> 5) & 3
        for k in range(4):
            rk_ref[k * 64 : k * 64 + 64, :] = jnp.where(part == k, spread, jnp.zeros_like(spread))
        keep = keep_of(meta_ref, q, 256)
        for r_hi in range(2):
            rows = jnp.concatenate(
                [y_ref[i * 256 + k * 64 : i * 256 + k * 64 + 64, r_hi * WIDE : r_hi * WIDE + WIDE] for k in range(4)],
                axis=1,
            )
            applied = dot(rows, rk_ref[...], ((1,), (1,)))
            state = bond_ref[q, :, r_hi * 256 : r_hi * 256 + 256].astype(f32)
            trial = jnp.where(keep, state - relax_step * applied, 0.0)
            total_ref[...] += trial * trial
            state_ref[q + 1, :, r_hi * 256 : r_hi * 256 + 256] = (trial * lift_scale).astype(bf16)


def handed_sector(meta_ref, q, left, state_ref, x_ref):
    lift_into(meta_ref, q, left, state_ref, x_ref)
    own = state_ref[q + 1]
    stacked = jnp.concatenate([own[:, k * 128 : k * 128 + 128] for k in range(4)], axis=0)
    both = dot(stacked, x_ref[:256, :], ((0,), (0,)))
    low = iota((BS, 128), 1) < 64
    out = []
    for w in range(0, W, 2):
        a0, b0 = both[:64, w * 128 : w * 128 + 128], both[64:, w * 128 : w * 128 + 128]
        a1, b1 = both[:64, w * 128 + 128 : w * 128 + 256], both[64:, w * 128 + 128 : w * 128 + 256]
        out.append(jnp.where(low, a0, b1) + pltpu.roll(jnp.where(low, a1, b0), 64, 1))
    return jnp.concatenate(out, axis=1)


def kernel(segs, blks, count, meta_in, bond_in, left_in, right_in, mpo_ref, out_ref,
           meta_land, meta_ref, bond_ref, left_ref, right_ref, spread_ref, ordered_ref, state_ref,
           halo_ref, lane_ref, order_ref, mix_ref, x_ref, y_ref, rk_ref, total_ref, sums_ref, raw_ref,
           local_sem, bond_send, bond_recv, left_send, left_recv, meta_sem, halo_send, halo_recv, sum_send, sum_recv):
    seg, blk = lax.axis_index("seg"), lax.axis_index("blk")
    ahead, behind = lax.rem(seg + 1, segs), lax.rem(seg + segs - 1, segs)
    up, down = lax.rem(blk + 1, blks), lax.rem(blk + blks - 1, blks)
    sectors = bond_ref.shape[0]
    groups = sectors // 2

    def remote(src, dst, send, recv, where):
        return pltpu.make_async_remote_copy(
            src_ref=src, dst_ref=dst, send_sem=send, recv_sem=recv, device_id=where,
            device_id_type=pl.DeviceIdType.MESH,
        )

    def bond_copy(g):
        part = pl.ds(g * 2, 2)
        return remote(bond_in.at[part], bond_ref.at[part], bond_send.at[g], bond_recv.at[g], {"seg": ahead})

    def left_copy(g):
        part = pl.ds(g * 2, 2)
        return remote(left_in.at[part], left_ref.at[part], left_send.at[g], left_recv.at[g], {"seg": ahead})

    def halo_copy(i, src):
        return remote(src, halo_ref.at[i], halo_send.at[i], halo_recv.at[i], {"blk": up if i % 2 == 0 else down})

    def sum_copy(k):
        return remote(sums_ref.at[0], sums_ref.at[k], sum_send.at[k], sum_recv.at[k], {"blk": lax.rem(blk + k, blks)})

    barrier = pltpu.get_barrier_semaphore()
    for where in [{"seg": ahead}, {"seg": behind}] + [{"blk": lax.rem(blk + k, blks)} for k in range(1, blks)]:
        pl.semaphore_signal(barrier, inc=1, device_id=where, device_id_type=pl.DeviceIdType.MESH)
    pl.semaphore_wait(barrier, blks + 1)

    meta_copy = remote(meta_in, meta_land, meta_sem.at[0], meta_sem.at[1], {"seg": ahead})
    meta_copy.start()
    bond_copy(groups - 1).start()
    bond_copy(0).start()
    bond_copy(1).start()
    left_copy(0).start()
    bond_copy(2).start()
    left_copy(1).start()
    right_copy = pltpu.make_async_copy(right_in, right_ref, local_sem.at[0])
    right_copy.start()
    order_state(lane_ref)
    total_ref[...] = jnp.zeros_like(total_ref)
    meta_copy.wait_recv()
    to_smem = pltpu.make_async_copy(meta_land, meta_ref, local_sem.at[1])
    to_smem.start()
    to_smem.wait()

    def prepare(g):
        for i in range(2):
            q = g * 2 + i
            held = jnp.where(keep_of(meta_ref, q, LANES), bond_ref[q].astype(f32), 0.0).astype(bf16)
            ordered_ref[q + 1] = dot(held, lane_ref[...]).astype(bf16)

    bond_copy(groups - 1).wait_recv()
    prepare(groups - 1)
    first = halo_copy(0, ordered_ref.at[sectors])
    first.start()
    bond_copy(0).wait_recv()
    prepare(0)
    last = halo_copy(1, ordered_ref.at[1])
    last.start()
    spread_operator(mpo_ref, mix_ref)
    order_right(order_ref)
    right_copy.wait()

    def spread_right(q, carry):
        spread_ref[q] = dot(right_ref[q], order_ref[...]).astype(bf16)
        return carry

    lax.fori_loop(0, sectors, spread_right, 0)
    first.wait_recv()
    last.wait_recv()
    low_edge = (blk > 0).astype(f32)
    high_edge = (blk < blks - 1).astype(f32)
    ordered_ref[0] = (halo_ref[0].astype(f32) * low_edge).astype(bf16)
    ordered_ref[sectors + 1] = (halo_ref[1].astype(f32) * high_edge).astype(bf16)

    def handed_pair(g):
        for i in range(2):
            q = g * 2 + i
            raw_ref[q] = handed_sector(meta_ref, q, left_ref[q], state_ref, x_ref)

    def step(g, carry):
        @pl.when(g + 3 < groups - 1)
        def _():
            bond_copy(g + 3).start()

        @pl.when(g + 2 < groups)
        def _():
            left_copy(g + 2).start()

        @pl.when(g + 1 < groups - 1)
        def _():
            bond_copy(g + 1).wait_recv()
            prepare(g + 1)

        left_copy(g).wait_recv()
        relax_pair(meta_ref, g, left_ref, spread_ref, bond_ref, ordered_ref, mix_ref, x_ref, y_ref, rk_ref,
                   state_ref, total_ref)

        @pl.when(g == 0)
        def _():
            halo_copy(3, state_ref.at[1]).start()

        @pl.when(g == groups - 1)
        def _():
            halo_copy(2, state_ref.at[sectors]).start()
            total = total_ref[...]
            part = total[:, :128] + total[:, 128:]
            sums_ref[0] = sum(part[k * 8 : k * 8 + 8] for k in range(8))
            for k in range(1, blks):
                sum_copy(k).start()

        @pl.when(g >= 2)
        def _():
            handed_pair(g - 1)

        return carry

    lax.fori_loop(0, groups, step, 0)
    third, fourth = halo_copy(2, state_ref.at[sectors]), halo_copy(3, state_ref.at[1])
    third.wait_recv()
    fourth.wait_recv()
    state_ref[0] = (halo_ref[2].astype(f32) * low_edge).astype(bf16)
    state_ref[sectors + 1] = (halo_ref[3].astype(f32) * high_edge).astype(bf16)
    lax.fori_loop(0, 2, lambda i, carry: (handed_pair((groups - 1) * (1 - i)), carry)[1], 0)
    for k in range(1, blks):
        sum_copy(k).wait_recv()
    total = sums_ref[0]
    for k in range(1, blks):
        total += sums_ref[k]
    mean_square = jnp.sum(jnp.sum(total, axis=1, keepdims=True), axis=0, keepdims=True) / count
    scale = 1.0 / ((mean_square + epsilon) * (lift_scale * lift_scale * math.sqrt(BS * P_SIZE)))

    def finish(q, carry):
        out_ref[q] = (raw_ref[q] * scale).astype(bf16)
        return carry

    lax.fori_loop(0, sectors, finish, 0)
    meta_copy.wait_send()
    for copy in (first, last, third, fourth):
        copy.wait_send()
    for k in range(1, blks):
        sum_copy(k).wait_send()

    def drain(g, carry):
        bond_copy(g).wait_send()
        left_copy(g).wait_send()
        return carry

    lax.fori_loop(0, groups, drain, 0)


def shards(bond_tensor, left_env, right_env, kept_dims, sector_links, mpo_pair):
    segs, blks = lax.axis_size("seg"), lax.axis_size("blk")
    sectors = left_env.shape[1]
    meta = jnp.concatenate([sector_links[0], kept_dims[0].T], axis=1)
    meta = jnp.pad(meta, ((0, 0), (0, 128 - W - 2)))
    count = sectors * blks * BS * P_SIZE * BS
    anywhere = pl.BlockSpec(memory_space=pl.ANY)
    vmem = pl.BlockSpec(memory_space=pltpu.VMEM)
    dma = pltpu.SemaphoreType.DMA
    out = pl.pallas_call(
        functools.partial(kernel, segs, blks, count),
        out_shape=jax.ShapeDtypeStruct((sectors, BS, WIDE), bf16),
        in_specs=[anywhere, anywhere, anywhere, anywhere, vmem],
        out_specs=vmem,
        scratch_shapes=[
            pltpu.VMEM((sectors, 128), jnp.int32),
            pltpu.SMEM((sectors, 128), jnp.int32),
            pltpu.VMEM((sectors, BS, LANES), bf16),
            pltpu.VMEM((sectors, BS, WIDE), bf16),
            pltpu.VMEM((sectors, BS, WIDE), bf16),
            pltpu.VMEM((sectors, BS, 4 * WIDE), bf16),
            pltpu.VMEM((sectors + 2, BS, LANES), bf16),
            pltpu.VMEM((sectors + 2, BS, LANES), bf16),
            pltpu.VMEM((4, BS, LANES), bf16),
            pltpu.VMEM((LANES, LANES), bf16),
            pltpu.VMEM((WIDE, 4 * WIDE), bf16),
            pltpu.VMEM((MIX, MIX), bf16),
            pltpu.VMEM((512, MIX), bf16),
            pltpu.VMEM((512, MIX), bf16),
            pltpu.VMEM((256, 4 * WIDE), bf16),
            pltpu.VMEM((BS, 256), f32),
            pltpu.VMEM((blks, 8, 128), f32),
            pltpu.VMEM((sectors, BS, WIDE), f32),
            dma((2,)),
            dma((sectors // 2,)),
            dma((sectors // 2,)),
            dma((sectors // 2,)),
            dma((sectors // 2,)),
            dma((2,)),
            dma((4,)),
            dma((4,)),
            dma((blks,)),
            dma((blks,)),
        ],
        compiler_params=pltpu.CompilerParams(
            collective_id=0, has_side_effects=True, vmem_limit_bytes=56 * 2**20
        ),
    )(meta, bond_tensor[0], left_env[0], right_env[0], mpo_pair)
    return out[None]


def solution(mesh):
    return jax.shard_map(
        shards,
        mesh=mesh,
        in_specs=(
            P(("runs", "seg"), "blk", None, None),
            P(("runs", "seg"), "blk", None, None),
            P(("runs", "seg"), "blk", None, None),
            P(("runs", "seg"), None, "blk"),
            P(("runs", "seg"), "blk", None),
            P(),
        ),
        out_specs=P(("runs", "seg"), "blk", None, None),
        check_vma=False,
    )
```

time: 145 us -> 79.6 us (0.55)
  waiting for transfers between devices: 52.7 us -> 0 us
  starting transfers between devices: 21 us -> 0 us
  Pallas kernels: 60.8 us -> 74.7 us
  blocking collectives: 7.38 us -> 0 us
  local copies, waits for them, and re-layouts: 0.86 us -> 4.61 us
    ppermute x10 -> x0, waiting for transfers between devices: 52.7 us -> none  [the longest x1 49.7 us: shards(): kept = padded(lax.ppermute(kept_dims[0], 'seg', ring), 1)]
    ppermute x10 -> x0, starting transfers between devices: 21 us -> none  [the longest x3 10.9 us: padded(): lax.ppermute(lax.slice_in_dim(block, size - 1, None, axis=dim), 'blk', fo...]
    pallas_call x2 -> x1, Pallas kernels: 60.8 us -> 74.7 us  [shards(): pl.pallas_call(functools.partial(kernel, segs, blks, count), out_shape=ja...]
    psum x1 -> x0, blocking collectives: 7.38 us -> none  [shards(): mean_square = lax.psum(jnp.sum(total), 'blk') / total_count]
    unnamed x5 -> x2, local copies, waits for them, and re-layouts: 0.77 us -> 3.25 us
  transfers between devices with their start and end apart: 10 -> 0, of which waited for: 2 -> 0; matrix products, arithmetic and copies ran while one was open for 1% -> 0% of each run, Pallas kernels for 0% -> 0%
where the time goes in v2:
time: 79.6 us; the launch traced here: 79.4 us
  Pallas kernels  74.7 us (94%)
  local copies, waits for them, and re-layouts  4.61 us (6%)
    pallas_call x1, Pallas kernels, shards(): pl.pallas_call(functools.partial(kernel, segs, blks, count), out_shape=ja...  74.7 us
    unnamed x2, local copies, waits for them, and re-layouts  3.25 us

profile of v2, /device:TPU:0, one launch (start us, length us, event | category | flops | bytes accessed | tf_op | source)
XLA Modules:
  0.0 79.4 jit_solution(14441832563162685941)
XLA Ops:
  0.0 0.8 copy.8
  0.8 0.8 copy.7
  1.5 0.1 pad_add_fusion
  1.6 0.6 pad.4.meta_in
  2.2 74.7 %shard_map.64 = bf16[16,64,640]{2,1,0:T(8,128)(2,1)} custom-call(s32[16,128]{1,0:T(8,128)} %pad.4.meta_in, bf16[16,64,512]{2,1,0:T(8,128)(2,1)} %bitcast.10, bf16[16,64,640]{2,1,0:T(8,128)(2,1)} %bitcast.8, bf16[16,64,640]{2,1,0:T(8,128)(2,1)} %bitcast.9, bf16[80,80]{1,0:T(8,128)(2,1)} %mpo_ref.1), custom_call_target="tpu_custom_call" | custom-call | tf_op jit(solution)/shard_map/pallas_call | solution.py:282
  76.9 2.5 %copy.10 = bf16[1,16,64,640]{3,2,1,0:T(8,128)(2,1)} copy(bf16[1,16,64,640]{3,2,1,0:T(8,128)(2,1)} %bitcast.7) | data formatting | bytes 2621440

commit v3 on v2

--- a/solution.py
+++ b/solution.py
@@ -66,18 +66,29 @@
     return rows & columns
 
 
-def lift_into(meta_ref, q, left, state_ref, target_ref, base=0):
+def place_left(meta_ref, q, left_ref, block_ref):
+    half = iota((BS, 256), 1) >> 6
     for w in range(W):
-        source = state_ref[q + 1 + meta_ref[q, w]]
-        out = dot(left[:, w * 64 : w * 64 + 64], source).astype(bf16)
+        piece = left_ref[q, :, w * 64 : w * 64 + 64]
+        wide = jnp.concatenate([piece] * 4, axis=1)
+        block_ref[q, w * 64 : w * 64 + 64, :] = jnp.where(half == meta_ref[q, w] + 1, wide, jnp.zeros_like(wide))
+
+
+def lift_into(q, block_ref, state_ref, target_ref, base=0):
+    source = state_ref[pl.ds(q, 3)].reshape(3 * BS, LANES)
+    out = dot(block_ref[q, :, :192], source).astype(bf16)
+    for w in range(W):
         for k in range(4):
-            target_ref[base + k * 64 : base + k * 64 + 64, w * 128 : w * 128 + 128] = out[:, k * 128 : k * 128 + 128]
-
-
-def relax_pair(meta_ref, g, left_ref, spread_ref, bond_ref, ordered_ref, mix_ref, x_ref, y_ref, rk_ref, state_ref, total_ref):
+            target_ref[base + k * 64 : base + k * 64 + 64, w * 128 : w * 128 + 128] = (
+                out[w * 64 : w * 64 + 64, k * 128 : k * 128 + 128]
+            )
+
+
+def relax_pair(meta_ref, g, left_ref, block_ref, spread_ref, bond_ref, ordered_ref, mix_ref, x_ref, y_ref, rk_ref, state_ref, total_ref):
     for i in range(2):
         q = g * 2 + i
-        lift_into(meta_ref, q, left_ref[q], ordered_ref, x_ref, i * 256)
+        place_left(meta_ref, q, left_ref, block_ref)
+        lift_into(q, block_ref, ordered_ref, x_ref, i * 256)
     y_ref[...] = dot(x_ref[...], mix_ref[...]).astype(bf16)
     for i in range(2):
         q = g * 2 + i
@@ -86,20 +97,24 @@
         for k in range(4):
             rk_ref[k * 64 : k * 64 + 64, :] = jnp.where(part == k, spread, jnp.zeros_like(spread))
         keep = keep_of(meta_ref, q, 256)
-        for r_hi in range(2):
-            rows = jnp.concatenate(
+        rows = [
+            jnp.concatenate(
                 [y_ref[i * 256 + k * 64 : i * 256 + k * 64 + 64, r_hi * WIDE : r_hi * WIDE + WIDE] for k in range(4)],
                 axis=1,
             )
-            applied = dot(rows, rk_ref[...], ((1,), (1,)))
+            for r_hi in range(2)
+        ]
+        both = dot(jnp.concatenate(rows, axis=0), rk_ref[...], ((1,), (1,)))
+        for r_hi in range(2):
+            applied = both[r_hi * 64 : r_hi * 64 + 64]
             state = bond_ref[q, :, r_hi * 256 : r_hi * 256 + 256].astype(f32)
             trial = jnp.where(keep, state - relax_step * applied, 0.0)
             total_ref[...] += trial * trial
             state_ref[q + 1, :, r_hi * 256 : r_hi * 256 + 256] = (trial * lift_scale).astype(bf16)
 
 
-def handed_sector(meta_ref, q, left, state_ref, x_ref):
-    lift_into(meta_ref, q, left, state_ref, x_ref)
+def handed_sector(q, block_ref, state_ref, x_ref):
+    lift_into(q, block_ref, state_ref, x_ref)
     own = state_ref[q + 1]
     stacked = jnp.concatenate([own[:, k * 128 : k * 128 + 128] for k in range(4)], axis=0)
     both = dot(stacked, x_ref[:256, :], ((0,), (0,)))
@@ -112,9 +127,9 @@
     return jnp.concatenate(out, axis=1)
 
 
-def kernel(segs, blks, count, meta_in, bond_in, left_in, right_in, mpo_ref, out_ref,
+def kernel(segs, blks, count, meta_in, bond_in, left_in, right_in, mpo_ref, raw_ref, scale_ref,
            meta_land, meta_ref, bond_ref, left_ref, right_ref, spread_ref, ordered_ref, state_ref,
-           halo_ref, lane_ref, order_ref, mix_ref, x_ref, y_ref, rk_ref, total_ref, sums_ref, raw_ref,
+           halo_ref, lane_ref, order_ref, mix_ref, x_ref, y_ref, rk_ref, total_ref, sums_ref, block_ref,
            local_sem, bond_send, bond_recv, left_send, left_recv, meta_sem, halo_send, halo_recv, sum_send, sum_recv):
     seg, blk = lax.axis_index("seg"), lax.axis_index("blk")
     ahead, behind = lax.rem(seg + 1, segs), lax.rem(seg + segs - 1, segs)
@@ -194,10 +209,8 @@
     ordered_ref[0] = (halo_ref[0].astype(f32) * low_edge).astype(bf16)
     ordered_ref[sectors + 1] = (halo_ref[1].astype(f32) * high_edge).astype(bf16)
 
-    def handed_pair(g):
-        for i in range(2):
-            q = g * 2 + i
-            raw_ref[q] = handed_sector(meta_ref, q, left_ref[q], state_ref, x_ref)
+    def hand(q):
+        raw_ref[q] = handed_sector(q, block_ref, state_ref, x_ref)
 
     def step(g, carry):
         @pl.when(g + 3 < groups - 1)
@@ -214,7 +227,7 @@
             prepare(g + 1)
 
         left_copy(g).wait_recv()
-        relax_pair(meta_ref, g, left_ref, spread_ref, bond_ref, ordered_ref, mix_ref, x_ref, y_ref, rk_ref,
+        relax_pair(meta_ref, g, left_ref, block_ref, spread_ref, bond_ref, ordered_ref, mix_ref, x_ref, y_ref, rk_ref,
                    state_ref, total_ref)
 
         @pl.when(g == 0)
@@ -230,9 +243,10 @@
             for k in range(1, blks):
                 sum_copy(k).start()
 
-        @pl.when(g >= 2)
-        def _():
-            handed_pair(g - 1)
+        @pl.when(g >= 1)
+        def _():
+            hand(g * 2 - 1)
+            hand(g * 2)
 
         return carry
 
@@ -242,7 +256,8 @@
     fourth.wait_recv()
     state_ref[0] = (halo_ref[2].astype(f32) * low_edge).astype(bf16)
     state_ref[sectors + 1] = (halo_ref[3].astype(f32) * high_edge).astype(bf16)
-    lax.fori_loop(0, 2, lambda i, carry: (handed_pair((groups - 1) * (1 - i)), carry)[1], 0)
+    hand(sectors - 1)
+    hand(0)
     for k in range(1, blks):
         sum_copy(k).wait_recv()
     total = sums_ref[0]
@@ -251,11 +266,7 @@
     mean_square = jnp.sum(jnp.sum(total, axis=1, keepdims=True), axis=0, keepdims=True) / count
     scale = 1.0 / ((mean_square + epsilon) * (lift_scale * lift_scale * math.sqrt(BS * P_SIZE)))
 
-    def finish(q, carry):
-        out_ref[q] = (raw_ref[q] * scale).astype(bf16)
-        return carry
-
-    lax.fori_loop(0, sectors, finish, 0)
+    scale_ref[...] = jnp.broadcast_to(scale, scale_ref.shape)
     meta_copy.wait_send()
     for copy in (first, last, third, fourth):
         copy.wait_send()
@@ -279,11 +290,11 @@
     anywhere = pl.BlockSpec(memory_space=pl.ANY)
     vmem = pl.BlockSpec(memory_space=pltpu.VMEM)
     dma = pltpu.SemaphoreType.DMA
-    out = pl.pallas_call(
+    raw, scale = pl.pallas_call(
         functools.partial(kernel, segs, blks, count),
-        out_shape=jax.ShapeDtypeStruct((sectors, BS, WIDE), bf16),
+        out_shape=(jax.ShapeDtypeStruct((sectors, BS, WIDE), f32), jax.ShapeDtypeStruct((8, 128), f32)),
         in_specs=[anywhere, anywhere, anywhere, anywhere, vmem],
-        out_specs=vmem,
+        out_specs=(vmem, vmem),
         scratch_shapes=[
             pltpu.VMEM((sectors, 128), jnp.int32),
             pltpu.SMEM((sectors, 128), jnp.int32),
@@ -302,7 +313,7 @@
             pltpu.VMEM((256, 4 * WIDE), bf16),
             pltpu.VMEM((BS, 256), f32),
             pltpu.VMEM((blks, 8, 128), f32),
-            pltpu.VMEM((sectors, BS, WIDE), f32),
+            pltpu.VMEM((sectors, WIDE, 256), bf16),
             dma((2,)),
             dma((sectors // 2,)),
             dma((sectors // 2,)),
@@ -318,7 +329,7 @@
             collective_id=0, has_side_effects=True, vmem_limit_bytes=56 * 2**20
         ),
     )(meta, bond_tensor[0], left_env[0], right_env[0], mpo_pair)
-    return out[None]
+    return (raw * scale[0, 0]).astype(bf16)[None]
 
 
 def solution(mesh):

time: 79.6 us -> 81 us (1.018)
  other arithmetic: 0.08 us -> 3.67 us
  local copies, waits for them, and re-layouts: 4.61 us -> 3.31 us
  Pallas kernels: 74.7 us -> 73.7 us
    broadcast_in_dim x0 -> x1, other arithmetic: none -> 3.6 us  [shards(): return (raw * scale[0, 0]).astype(bf16)[None]]
    unnamed x2 -> x1, local copies, waits for them, and re-layouts: 3.25 us -> 0.76 us
    slice x0 -> x1, local copies, waits for them, and re-layouts: none -> 1.19 us  [shards(): return (raw * scale[0, 0]).astype(bf16)[None]]
    pallas_call x1, Pallas kernels: 74.7 us -> 73.7 us  [shards(): pl.pallas_call(functools.partial(kernel, segs, blks, count), out_shape=(j...]
where the time goes in v3:
time: 81 us; the launch traced here: 80.7 us
  Pallas kernels  73.7 us (91%)
  other arithmetic  3.67 us (5%)
  local copies, waits for them, and re-layouts  3.31 us (4%)
    pallas_call x1, Pallas kernels, shards(): pl.pallas_call(functools.partial(kernel, segs, blks, count), out_shape=(j...  73.7 us
    broadcast_in_dim x1, other arithmetic, shards(): return (raw * scale[0, 0]).astype(bf16)[None]  3.6 us

profile of v3, /device:TPU:0, one launch (start us, length us, event | category | flops | bytes accessed | tf_op | source)
XLA Modules:
  0.0 80.7 jit_solution(15574595971249864031)
XLA Ops:
  0.0 0.8 copy.8
  0.8 0.8 copy.7
  1.5 0.1 pad_add_fusion
  1.6 0.6 pad.4.meta_in
  2.2 73.7 %shard_map.64 = (f32[16,64,640]{2,1,0:T(8,128)}, f32[8,128]{1,0:T(8,128)}) custom-call(s32[16,128]{1,0:T(8,128)} %pad.4.meta_in, bf16[16,64,512]{2,1,0:T(8,128)(2,1)} %bitcast.11, bf16[16,64,640]{2,1,0:T(8,128)(2,1)} %bitcast.9, bf16[16,64,640]{2,1,0:T(8,128)(2,1)} %bitcast.10, bf16[80,80]{1,0:T(8,128)(2,1)} %mpo_ref.1), custom_call_target="tpu_custom_call" | custom-call | tf_op jit(solution)/shard_map/pallas_call | solution.py:293
  75.9 1.2 %slice.3 = f32[1,1]{1,0:T(1,128)} slice(f32[8,128]{1,0:T(8,128)} %get-tuple-element.8), slice={[0:1], [0:1]} | slice | bytes 8 | tf_op jit(solution)/shard_map/slice | solution.py:332
  77.1 3.6 %fusion = bf16[1,16,64,640]{3,2,1,0:T(8,128)(2,1)} fusion(f32[16,64,640]{2,1,0:T(8,128)} %get-tuple-element.7, f32[]{:T(128)} %bitcast.6), kind=kLoop, calls=%fused_computation.1 | loop fusion | flops 1310720 | bytes 3932164 | tf_op jit(solution)/shard_map/broadcast_in_dim | solution.py:332

commit v4 on v3

--- a/solution.py
+++ b/solution.py
@@ -127,9 +127,9 @@
     return jnp.concatenate(out, axis=1)
 
 
-def kernel(segs, blks, count, meta_in, bond_in, left_in, right_in, mpo_ref, raw_ref, scale_ref,
+def kernel(segs, blks, count, meta_in, bond_in, left_in, right_in, mpo_ref, out_ref,
            meta_land, meta_ref, bond_ref, left_ref, right_ref, spread_ref, ordered_ref, state_ref,
-           halo_ref, lane_ref, order_ref, mix_ref, x_ref, y_ref, rk_ref, total_ref, sums_ref, block_ref,
+           halo_ref, lane_ref, order_ref, mix_ref, x_ref, y_ref, rk_ref, total_ref, sums_ref, block_ref, raw_ref,
            local_sem, bond_send, bond_recv, left_send, left_recv, meta_sem, halo_send, halo_recv, sum_send, sum_recv):
     seg, blk = lax.axis_index("seg"), lax.axis_index("blk")
     ahead, behind = lax.rem(seg + 1, segs), lax.rem(seg + segs - 1, segs)
@@ -174,6 +174,15 @@
     right_copy.start()
     order_state(lane_ref)
     total_ref[...] = jnp.zeros_like(total_ref)
+    spread_operator(mpo_ref, mix_ref)
+    order_right(order_ref)
+    right_copy.wait()
+
+    def spread_right(q, carry):
+        spread_ref[q] = dot(right_ref[q], order_ref[...]).astype(bf16)
+        return carry
+
+    lax.fori_loop(0, sectors, spread_right, 0)
     meta_copy.wait_recv()
     to_smem = pltpu.make_async_copy(meta_land, meta_ref, local_sem.at[1])
     to_smem.start()
@@ -193,15 +202,6 @@
     prepare(0)
     last = halo_copy(1, ordered_ref.at[1])
     last.start()
-    spread_operator(mpo_ref, mix_ref)
-    order_right(order_ref)
-    right_copy.wait()
-
-    def spread_right(q, carry):
-        spread_ref[q] = dot(right_ref[q], order_ref[...]).astype(bf16)
-        return carry
-
-    lax.fori_loop(0, sectors, spread_right, 0)
     first.wait_recv()
     last.wait_recv()
     low_edge = (blk > 0).astype(f32)
@@ -266,7 +266,12 @@
     mean_square = jnp.sum(jnp.sum(total, axis=1, keepdims=True), axis=0, keepdims=True) / count
     scale = 1.0 / ((mean_square + epsilon) * (lift_scale * lift_scale * math.sqrt(BS * P_SIZE)))
 
-    scale_ref[...] = jnp.broadcast_to(scale, scale_ref.shape)
+
+    def finish(q, carry):
+        out_ref[q] = (raw_ref[q] * scale).astype(bf16)
+        return carry
+
+    lax.fori_loop(0, sectors, finish, 0)
     meta_copy.wait_send()
     for copy in (first, last, third, fourth):
         copy.wait_send()
@@ -290,11 +295,11 @@
     anywhere = pl.BlockSpec(memory_space=pl.ANY)
     vmem = pl.BlockSpec(memory_space=pltpu.VMEM)
     dma = pltpu.SemaphoreType.DMA
-    raw, scale = pl.pallas_call(
+    out = pl.pallas_call(
         functools.partial(kernel, segs, blks, count),
-        out_shape=(jax.ShapeDtypeStruct((sectors, BS, WIDE), f32), jax.ShapeDtypeStruct((8, 128), f32)),
+        out_shape=jax.ShapeDtypeStruct((sectors, BS, WIDE), bf16),
         in_specs=[anywhere, anywhere, anywhere, anywhere, vmem],
-        out_specs=(vmem, vmem),
+        out_specs=vmem,
         scratch_shapes=[
             pltpu.VMEM((sectors, 128), jnp.int32),
             pltpu.SMEM((sectors, 128), jnp.int32),
@@ -314,6 +319,7 @@
             pltpu.VMEM((BS, 256), f32),
             pltpu.VMEM((blks, 8, 128), f32),
             pltpu.VMEM((sectors, WIDE, 256), bf16),
+            pltpu.VMEM((sectors, BS, WIDE), f32),
             dma((2,)),
             dma((sectors // 2,)),
             dma((sectors // 2,)),
@@ -329,7 +335,7 @@
             collective_id=0, has_side_effects=True, vmem_limit_bytes=56 * 2**20
         ),
     )(meta, bond_tensor[0], left_env[0], right_env[0], mpo_pair)
-    return (raw * scale[0, 0]).astype(bf16)[None]
+    return out[None]
 
 
 def solution(mesh):

time: 81 us -> 75.3 us (0.930)
  other arithmetic: 3.67 us -> 0.08 us
  Pallas kernels: 73.7 us -> 70.3 us
  local copies, waits for them, and re-layouts: 3.31 us -> 4.61 us
    broadcast_in_dim x1 -> x0, other arithmetic: 3.6 us -> none  [shards(): return (raw * scale[0, 0]).astype(bf16)[None]]
    pallas_call x1, Pallas kernels: 73.7 us -> 70.3 us  [shards(): pl.pallas_call(functools.partial(kernel, segs, blks, count), out_shape=ja...]
    unnamed x1 -> x2, local copies, waits for them, and re-layouts: 0.76 us -> 3.25 us
    slice x1 -> x0, local copies, waits for them, and re-layouts: 1.19 us -> none  [shards(): return (raw * scale[0, 0]).astype(bf16)[None]]
where the time goes in v4:
time: 75.3 us; the launch traced here: 75 us
  Pallas kernels  70.3 us (93%)
  local copies, waits for them, and re-layouts  4.61 us (6%)
    pallas_call x1, Pallas kernels, shards(): pl.pallas_call(functools.partial(kernel, segs, blks, count), out_shape=ja...  70.3 us
    unnamed x2, local copies, waits for them, and re-layouts  3.25 us

profile of v4, /device:TPU:0, one launch (start us, length us, event | category | flops | bytes accessed | tf_op | source)
XLA Modules:
  0.0 75.0 jit_solution(827948560372532613)
XLA Ops:
  0.0 0.8 %copy.8 = s32[2,16]{0,1:T(8,128)S(1)} copy(s32[2,16]{1,0:T(2,128)} %bitcast.13) | data formatting | bytes 256 | tf_op jit(solution)/shard_map/squeeze | solution.py:292
  0.8 0.8 %copy.7 = s32[1,16,10]{2,1,0:T(8,128)S(1)} copy(s32[1,16,10]{1,0,2:T(1,128)} %param.10) | data formatting | bytes 1280 | tf_op args[4]
  1.5 0.1 pad_add_fusion
  1.6 0.6 pad.4.meta_in
  2.2 70.3 %shard_map.64 = bf16[16,64,640]{2,1,0:T(8,128)(2,1)} custom-call(s32[16,128]{1,0:T(8,128)} %pad.4.meta_in, bf16[16,64,512]{2,1,0:T(8,128)(2,1)} %bitcast.10, bf16[16,64,640]{2,1,0:T(8,128)(2,1)} %bitcast.8, bf16[16,64,640]{2,1,0:T(8,128)(2,1)} %bitcast.9, bf16[80,80]{1,0:T(8,128)(2,1)} %mpo_ref.1), custom_call_target="tpu_custom_call" | custom-call | tf_op jit(solution)/shard_map/pallas_call | solution.py:298
  72.5 2.5 %copy.10 = bf16[1,16,64,640]{3,2,1,0:T(8,128)(2,1)} copy(bf16[1,16,64,640]{3,2,1,0:T(8,128)(2,1)} %bitcast.7) | data formatting | bytes 2621440
